TPU v7x, 32 devices: a whole 2x2x4 slice. The times are simulated.
32 devices in a mesh: rows: 4 (over y, x), cols: 8 (over z, core).
Axes of the slice: x: 2, y: 2, z: 4, core: 2. Of those that a mesh axis runs over, the one named last changes fastest.
Arguments:
- c_eta: float32 [512, 2048], P('rows', 'cols'), may hold values from -4 to 4
- c_flux: float32 [2, 512, 2048], P(None, 'rows', 'cols'), may hold values from -150 to 150
- c_depth: float32 [512, 2048], P('rows', 'cols'), may hold values from 100 to 4000
- f_bed: float32 [128, 2048], P('rows', 'cols'), may hold values from -3 to 1
- f_depth: float32 [128, 2048], P('rows', 'cols'), may hold values from 0.05 to 3
- f_wet: int32 [128, 2048], P('rows', 'cols'), may hold values 0 or 1
- f_class: int32 [128, 2048], P('rows', 'cols'), may hold values from 0 to 10
- manning: float32 [11], replicated, may hold values from 0.02 to 0.2
- nest_map: int32 [2048], replicated, may hold values from 0 to 1048575, as said below
Outputs:
- c_eta_out: float32 [512, 2048], P('rows', 'cols')
- f_water: float32 [128, 2048], P('rows', 'cols')
- f_flux: float32 [2, 128, 2048], P(None, 'rows', 'cols')
Inputs may be any that keep to these rules, and one draw needn't show every extreme that they name: `nest_map`: entry b is the flat index, row times 2048 plus column, of the coarse cell that drives fine boundary cell b; entries with the same b // 18 are equal; for s = b // 18 the coarse row lies in [(s * 128) % 512, (s * 128) % 512 + 128) and the coarse column is min(s * 18 * 1 + 256 + j, 2047) for some j in 0..128.
All inputs are finite; a program needn't handle non-finite values. No bound on the sum of `f_wet` on one device may be relied on, other than what follows from the above.
Results may differ from a plain program's by a relative error of at most 0.00002.
Values sent between devices are 32-bit elements; how exact they have to be, the bound alone decides.
A program may use at most 64 MiB of HBM per device.

v0:
```python
import jax
import jax.numpy as jnp
from jax import lax
from jax.sharding import PartitionSpec as P

NCLASS = 11
CSTEPS = 2
SUB = 3
FSTEPS = 6


gravity = 9.81
coarse_spacing = 90.0
coarse_tick = 0.25
fine_spacing = 5.0
depth_floor = 0.01
dry_depth = 0.05


def padded_2(block, sides, width):
    for axis, dim in sides:
        count = lax.axis_size(axis)
        forward = [(i, i + 1) for i in range(count - 1)]
        backward = [(target, source) for source, target in forward]
        low = lax.ppermute(
            lax.slice_in_dim(block, block.shape[dim] - width, None, axis=dim), axis, forward
        )
        high = lax.ppermute(lax.slice_in_dim(block, 0, width, axis=dim), axis, backward)
        block = jnp.concatenate([low, block, high], axis=dim)
    return block


def coarse_update(padded):
    surf = padded[0]
    total = padded[1]
    rows_flux = padded[2]
    cols_flux = padded[3]
    face_rows = jnp.minimum(total[:-1, 1:-1], total[1:, 1:-1])
    new_rows = jnp.minimum(face_rows, 1.0) * (
        rows_flux[:-1, 1:-1]
        - coarse_tick * gravity * face_rows * (surf[1:, 1:-1] - surf[:-1, 1:-1]) / coarse_spacing
    )
    face_cols = jnp.minimum(total[1:-1, :-1], total[1:-1, 1:])
    new_cols = jnp.minimum(face_cols, 1.0) * (
        cols_flux[1:-1, :-1]
        - coarse_tick * gravity * face_cols * (surf[1:-1, 1:] - surf[1:-1, :-1]) / coarse_spacing
    )
    surface = surf[1:-1, 1:-1] - coarse_tick / coarse_spacing * (
        new_rows[1:] - new_rows[:-1] + (new_cols[:, 1:] - new_cols[:, :-1])
    )
    return (surface, new_rows[1:], new_cols[:, 1:])


def face_flux(flux_old, face_depth, slope, rough, fine_tick):
    wetness = jnp.minimum(face_depth / dry_depth, 1.0)
    driven = flux_old - fine_tick * gravity * face_depth * slope / fine_spacing
    friction = 1.0 + fine_tick * gravity * rough * rough * jnp.abs(flux_old) / jnp.power(
        jnp.maximum(face_depth, depth_floor), 7.0 / 3.0
    )
    return wetness * driven / friction


def fine_faces(water_pad, bed_pad, rough_pad, rows_pad, cols_pad, fine_tick):
    surf = bed_pad + water_pad
    depth_rows = jnp.maximum(
        jnp.maximum(surf[:-1, 1:-1], surf[1:, 1:-1])
        - jnp.maximum(bed_pad[:-1, 1:-1], bed_pad[1:, 1:-1]),
        0.0,
    )
    rough_rows = 0.5 * (rough_pad[:-1, 1:-1] + rough_pad[1:, 1:-1])
    new_rows = face_flux(
        rows_pad[:-1, 1:-1], depth_rows, surf[1:, 1:-1] - surf[:-1, 1:-1], rough_rows, fine_tick
    )
    depth_cols = jnp.maximum(
        jnp.maximum(surf[1:-1, :-1], surf[1:-1, 1:])
        - jnp.maximum(bed_pad[1:-1, :-1], bed_pad[1:-1, 1:]),
        0.0,
    )
    rough_cols = 0.5 * (rough_pad[1:-1, :-1] + rough_pad[1:-1, 1:])
    new_cols = face_flux(
        cols_pad[1:-1, :-1], depth_cols, surf[1:-1, 1:] - surf[1:-1, :-1], rough_cols, fine_tick
    )
    return (new_rows, new_cols)


def open_boundary(water_top, bed_top, bnd_surface, bnd_velocity):
    return water_top * bnd_velocity + jnp.sqrt(gravity * jnp.maximum(water_top, depth_floor)) * (
        bnd_surface - (bed_top + water_top)
    )


def blend(levels_stack, fine_index):
    lower = fine_index // SUB
    weight = (fine_index % SUB + 1) / SUB
    return (1.0 - weight) * levels_stack[lower] + weight * levels_stack[lower + 1]


def per_device(c_eta, c_flux, c_depth, f_bed, f_depth, f_wet, f_class, manning, nest_map):
    row_index = lax.axis_index("rows")
    col_index = lax.axis_index("cols")
    row_count = lax.axis_size("rows")
    col_count = lax.axis_size("cols")
    tile_rows, tile_cols = c_eta.shape
    fine_rows_dev, fine_cols_dev = f_bed.shape
    coarse_width = tile_cols * col_count
    coarse_row = nest_map // coarse_width
    coarse_col = nest_map % coarse_width
    local_row = coarse_row - row_index * tile_rows
    local_col = coarse_col - col_index * tile_cols
    owned = (local_row >= 0) & (local_row < tile_rows) & (local_col >= 0) & (local_col < tile_cols)
    flat_index = jnp.where(owned, local_row * tile_cols + local_col, 0)
    owned_weight = jnp.where(owned, 1.0, 0.0)

    def sample(surface, rows_flux):
        velocity = rows_flux / (c_depth + surface)
        return jnp.stack(
            [
                jnp.take(surface.reshape(-1), flat_index) * owned_weight,
                jnp.take(velocity.reshape(-1), flat_index) * owned_weight,
            ]
        )

    surface = c_eta
    rows_flux = c_flux[0]
    cols_flux = c_flux[1]
    sampled = [sample(surface, rows_flux)]
    for coarse_index in range(CSTEPS):
        stacked = jnp.stack([surface, c_depth + surface, rows_flux, cols_flux])
        padded = padded_2(stacked, (("rows", 1), ("cols", 2)), 1)
        surface, rows_flux, cols_flux = coarse_update(padded)
        sampled.append(sample(surface, rows_flux))
    levels_stack = jnp.stack(sampled)
    per_step = jnp.stack([blend(levels_stack, fine_index) for fine_index in range(FSTEPS)])
    summed = lax.psum(per_step, ("rows", "cols"))
    boundary = lax.dynamic_slice_in_dim(summed, col_index * fine_cols_dev, fine_cols_dev, 2)
    roughness = jnp.zeros_like(f_bed)
    for class_index in range(NCLASS):
        roughness = jnp.where(f_class == class_index, manning[class_index], roughness)
    water = f_wet.astype(f_bed.dtype) * f_depth
    fine_rows = jnp.zeros_like(water)
    fine_cols = jnp.zeros_like(water)
    fine_tick = coarse_tick / SUB
    row_start = row_index * fine_rows_dev
    col_start = col_index * fine_cols_dev
    total_rows = fine_rows_dev * row_count
    total_cols = fine_cols_dev * col_count
    col_faces = col_start + jnp.arange(fine_cols_dev + 1)
    col_keep = jnp.where((col_faces == 0) | (col_faces == total_cols), 0.0, 1.0)[None, :]
    static_pad = padded_2(jnp.stack([f_bed, roughness]), (("rows", 1), ("cols", 2)), 1)
    bed_pad = static_pad[0]
    rough_pad = static_pad[1]
    row_faces = row_start + jnp.arange(fine_rows_dev + 1)
    row_keep = jnp.where(row_faces == total_rows, 0.0, 1.0)[:, None]
    at_top = row_index == 0
    for fine_index in range(FSTEPS):
        state_pad = padded_2(
            jnp.stack([water, fine_rows, fine_cols]), (("rows", 1), ("cols", 2)), 1
        )
        water_pad = state_pad[0]
        new_rows, new_cols = fine_faces(
            water_pad, bed_pad, rough_pad, state_pad[1], state_pad[2], fine_tick
        )
        new_rows = new_rows * row_keep
        new_cols = new_cols * col_keep
        top_flux = open_boundary(
            water_pad[1, 1:-1], bed_pad[1, 1:-1], boundary[fine_index, 0], boundary[fine_index, 1]
        )
        first_face = jnp.where(at_top, top_flux, new_rows[0])
        new_rows = jnp.concatenate([first_face[None, :], new_rows[1:]], axis=0)
        water = water_pad[1:-1, 1:-1] - fine_tick / fine_spacing * (
            new_rows[1:] - new_rows[:-1] + (new_cols[:, 1:] - new_cols[:, :-1])
        )
        fine_rows = new_rows[1:]
        fine_cols = new_cols[:, 1:]
    return (surface, water, jnp.stack([fine_rows, fine_cols]))


def solution(mesh):
    in_specs = (
        P("rows", "cols"),
        P(None, "rows", "cols"),
        P("rows", "cols"),
        P("rows", "cols"),
        P("rows", "cols"),
        P("rows", "cols"),
        P("rows", "cols"),
        P(),
        P(),
    )
    out_specs = (P("rows", "cols"), P("rows", "cols"), P(None, "rows", "cols"))
    return jax.shard_map(
        per_device, mesh=mesh, in_specs=in_specs, out_specs=out_specs, check_vma=False
    )
```

profile of v0, /device:TPU:0, one launch (start us, length us, event | category | flops | bytes accessed | tf_op | source)
XLA Modules:
  0.0 373.9 jit_solution(18096316524865931316)
XLA Ops:
  7.2 1.1 fusion.22
  8.4 4.8 %collective-permute-start = (f32[4,1,256]{2,1,0:T(1,128)S(1)}, f32[4,1,256]{2,1,0:T(1,128)S(1)}, u32[]{:S(2)}, u32[]{:S(2)}) collective-permute-start(f32[4,1,256]{2,1,0:T(1,128)S(1)} %get-tuple-element.32), channel_id=1, source_target_pairs={{0,8},{8,16},{16,24},{1,9},{9,17},{17,25},{2,10},{10,18},{18,26},{... | collective-permute-start | bytes 12296 | tf_op jit(solution)/shard_map/ppermute | solution.py:25
  13.3 1.3 collective-permute-start.1
  15.3 7.0 %select_bitcast_fusion = f32[1,32,256]{2,1,0:T(8,128)S(1)} fusion(s32[32,256]{1,0:T(8,128)S(1)} %copy-done.9, f32[]{:T(128)} %bitcast.27, f32[]{:T(128)} %bitcast.26, f32[]{:T(128)} %bitcast.25, f32[]{:T(128)} %bitcast.24, f32[]{:T(128)} %bitcast.23, f32[]{:T(128)} %bitcast.22, f32[]{:T(128)} %bitcast.21, f32[]{:T(128)} %bitcast.20, f32[]{:T(128)} %bitcast.19, ...), kind=kLoop, calls=%fused_computation.156 | loop fusion | flops 180224 | bytes 65580 | tf_op jit(solution)/shard_map/stack | solution.py:149
  22.3 4.5 %collective-permute-start.12 = (f32[2,1,256]{2,1,0:T(1,128)S(1)}, f32[2,1,256]{2,1,0:T(1,128)S(1)}, u32[]{:S(2)}, u32[]{:S(2)}) collective-permute-start(f32[2,1,256]{2,1,0:T(1,128)S(1)} %get-tuple-element.82), channel_id=1, source_target_pairs={{0,8},{8,16},{16,24},{1,9},{9,17},{17,25},{2,10},{10,18},{18,26},{... | collective-permute-start | bytes 6152 | tf_op jit(solution)/shard_map/ppermute | solution.py:25
  26.9 1.3 collective-permute-start.13
  28.2 4.9 %collective-permute-start.8 = (f32[3,1,256]{2,1,0:T(1,128)S(1)}, f32[3,1,256]{2,1,0:T(1,128)S(1)}, u32[]{:S(2)}, u32[]{:S(2)}) collective-permute-start(f32[3,1,256]{2,1,0:T(1,128)S(1)} %get-tuple-element.108), channel_id=1, source_target_pairs={{0,8},{8,16},{16,24},{1,9},{9,17},{17,25},{2,10},{10,18},{18,26},{... | collective-permute-start | bytes 9224 | tf_op jit(solution)/shard_map/ppermute | solution.py:25
  34.1 11.8 %gather_fusion.1 = f32[2048]{0:T(1024)S(1)} fusion(f32[32768]{0:T(1024)S(1)} %bitcast.271, s32[2048]{0:T(1024)S(1)} %get-tuple-element.10), kind=kCustom, calls=%fused_computation.1.clone | custom fusion | bytes 24576 | tf_op jit(solution)/shard_map/jit(_take)/gather | solution.py:119
  45.8 11.8 %gather_fusion = f32[2048]{0:T(1024)S(1)} fusion(f32[32768]{0:T(1024)S(1)} %bitcast.272, s32[2048]{0:T(1024)S(1)} %get-tuple-element.10), kind=kCustom, calls=%fused_computation.clone | custom fusion | bytes 24576 | tf_op jit(solution)/shard_map/jit(_take)/gather | solution.py:118
  57.8 1.3 collective-permute-start.14
  59.1 1.3 collective-permute-start.15
  60.4 1.3 collective-permute-start.9
  61.7 2.3 collective-permute-done.15
  64.1 2.6 collective-permute-done.9
  66.9 4.0 %collective-permute-start.10 = (f32[3,34,1]{2,1,0:T(8,128)S(1)}, f32[3,34,1]{2,1,0:T(8,128)S(1)}, u32[]{:S(2)}, u32[]{:S(2)}) collective-permute-start(f32[3,34,1]{2,1,0:T(8,128)S(1)} %get-tuple-element.68), channel_id=1, source_target_pairs={{0,1},{1,2},{2,3},{3,4},{4,5},{5,6},{6,7},{8,9},{9,10},{10,11},{11... | collective-permute-start | bytes 1232 | tf_op jit(solution)/shard_map/ppermute | solution.py:25
  70.8 1.3 collective-permute-start.11
  72.2 3.9 %collective-permute-done.11 = f32[3,34,1]{2,1,0:T(8,128)S(1)} collective-permute-done((f32[3,34,1]{2,1,0:T(8,128)S(1)}, f32[3,34,1]{2,1,0:T(8,128)S(1)}, u32[]{:S(2)}, u32[]{:S(2)}) %collective-permute-start.11) | collective-permute-done | bytes 440 | tf_op jit(solution)/shard_map/ppermute | solution.py:28
  76.5 4.8 %collective-permute-start.2 = (f32[4,130,1]{2,1,0:T(8,128)S(1)}, f32[4,130,1]{2,1,0:T(8,128)S(1)}, u32[]{:S(2)}, u32[]{:S(2)}) collective-permute-start(f32[4,130,1]{2,1,0:T(8,128)S(1)} %get-tuple-element.28), channel_id=1, source_target_pairs={{0,1},{1,2},{2,3},{3,4},{4,5},{5,6},{6,7},{8,9},{9,10},{10,11},{11... | collective-permute-start | bytes 6248 | tf_op jit(solution)/shard_map/ppermute | solution.py:25
  81.3 1.3 collective-permute-start.3
  82.7 2.1 collective-permute-done.3
  86.5 4.8 %collective-permute-start.4 = (f32[4,1,256]{2,1,0:T(1,128)S(1)}, f32[4,1,256]{2,1,0:T(1,128)S(1)}, u32[]{:S(2)}, u32[]{:S(2)}) collective-permute-start(f32[4,1,256]{2,1,0:T(1,128)S(1)} %get-tuple-element.30), channel_id=1, source_target_pairs={{0,8},{8,16},{16,24},{1,9},{9,17},{17,25},{2,10},{10,18},{18,26},{... | collective-permute-start | bytes 12296 | tf_op jit(solution)/shard_map/ppermute | solution.py:25
  91.4 1.3 collective-permute-start.5
  92.8 4.0 %collective-permute-done.5 = f32[4,1,256]{2,1,0:T(1,128)S(1)} collective-permute-done((f32[4,1,256]{2,1,0:T(1,128)S(1)}, f32[4,1,256]{2,1,0:T(1,128)S(1)}, u32[]{:S(2)}, u32[]{:S(2)}) %collective-permute-start.5) | collective-permute-done | bytes 4128 | tf_op jit(solution)/shard_map/ppermute | solution.py:28
  97.1 4.9 %collective-permute-start.6 = (f32[4,130,1]{2,1,0:T(8,128)S(1)}, f32[4,130,1]{2,1,0:T(8,128)S(1)}, u32[]{:S(2)}, u32[]{:S(2)}) collective-permute-start(f32[4,130,1]{2,1,0:T(8,128)S(1)} %get-tuple-element.26), channel_id=1, source_target_pairs={{0,1},{1,2},{2,3},{3,4},{4,5},{5,6},{6,7},{8,9},{9,10},{10,11},{11... | collective-permute-start | bytes 6248 | tf_op jit(solution)/shard_map/ppermute | solution.py:25
  102.0 1.3 collective-permute-start.7
  103.5 11.8 %gather_fusion.2 = f32[2048]{0:T(1024)S(1)} fusion(f32[32768]{0:T(1024)S(1)} %bitcast.275, s32[2048]{0:T(1024)S(1)} %get-tuple-element.10), kind=kCustom, calls=%fused_computation.2.clone | custom fusion | bytes 24576 | tf_op jit(solution)/shard_map/jit(_take)/gather | solution.py:118
  115.4 11.8 %gather_fusion.3 = f32[2048]{0:T(1024)S(1)} fusion(f32[32768]{0:T(1024)S(1)} %bitcast.274, s32[2048]{0:T(1024)S(1)} %get-tuple-element.10), kind=kCustom, calls=%fused_computation.3.clone | custom fusion | bytes 24576 | tf_op jit(solution)/shard_map/jit(_take)/gather | solution.py:119
  129.0 11.8 %gather_fusion.4 = f32[2048]{0:T(1024)S(1)} fusion(f32[32768]{0:T(1024)S(1)} %bitcast.276, s32[2048]{0:T(1024)S(1)} %get-tuple-element.10), kind=kCustom, calls=%fused_computation.4.clone | custom fusion | bytes 24576 | tf_op jit(solution)/shard_map/jit(_take)/gather | solution.py:118
  140.8 11.8 %gather_fusion.5 = f32[2048]{0:T(1024)S(1)} fusion(f32[32768]{0:T(1024)S(1)} %bitcast.273, s32[2048]{0:T(1024)S(1)} %get-tuple-element.10), kind=kCustom, calls=%fused_computation.5.clone | custom fusion | bytes 24576 | tf_op jit(solution)/shard_map/jit(_take)/gather | solution.py:119
  153.6 122.3 %all-reduce.3.cloned.1.call-done = f32[6,2,2048]{2,1,0:T(2,128)} async-done(((f32[6,2,2048]{2,1,0:T(2,128)}), f32[6,2,2048]{2,1,0:T(2,128)}) %all-reduce.3.cloned.1.call-update) | async-done | bytes 98320 | tf_op jit(solution)/shard_map/psum | solution.py:134
  276.9 3.4 collective-permute-start.16
  280.3 1.3 collective-permute-start.17
  281.6 4.2 %collective-permute-done.17 = f32[3,1,256]{2,1,0:T(1,128)S(1)} collective-permute-done((f32[3,1,256]{2,1,0:T(1,128)S(1)}, f32[3,1,256]{2,1,0:T(1,128)S(1)}, u32[]{:S(2)}, u32[]{:S(2)}) %collective-permute-start.17) | collective-permute-done | bytes 3104 | tf_op jit(solution)/shard_map/ppermute | solution.py:28
  285.9 1.3 collective-permute-start.18
  287.2 1.3 collective-permute-start.19
  288.5 5.3 %collective-permute-done.19 = f32[3,34,1]{2,1,0:T(8,128)S(1)} collective-permute-done((f32[3,34,1]{2,1,0:T(8,128)S(1)}, f32[3,34,1]{2,1,0:T(8,128)S(1)}, u32[]{:S(2)}, u32[]{:S(2)}) %collective-permute-start.19) | collective-permute-done | bytes 440 | tf_op jit(solution)/shard_map/ppermute | solution.py:28
  294.3 0.8 broadcast_select_fusion.4
  295.2 4.3 %collective-permute-start.20 = (f32[3,1,256]{2,1,0:T(1,128)S(1)}, f32[3,1,256]{2,1,0:T(1,128)S(1)}, u32[]{:S(2)}, u32[]{:S(2)}) collective-permute-start(f32[3,1,256]{2,1,0:T(1,128)S(1)} %get-tuple-element.76), channel_id=1, source_target_pairs={{0,8},{8,16},{16,24},{1,9},{9,17},{17,25},{2,10},{10,18},{18,26},{... | collective-permute-start | bytes 9224 | tf_op jit(solution)/shard_map/ppermute | solution.py:25
  299.5 1.3 collective-permute-start.21
  300.8 4.2 %collective-permute-done.21 = f32[3,1,256]{2,1,0:T(1,128)S(1)} collective-permute-done((f32[3,1,256]{2,1,0:T(1,128)S(1)}, f32[3,1,256]{2,1,0:T(1,128)S(1)}, u32[]{:S(2)}, u32[]{:S(2)}) %collective-permute-start.21) | collective-permute-done | bytes 3104 | tf_op jit(solution)/shard_map/ppermute | solution.py:28
  305.1 3.4 collective-permute-start.22
  308.5 1.3 collective-permute-start.23
  309.8 2.7 collective-permute-done.23
  314.0 2.8 collective-permute-start.24
  316.8 1.3 collective-permute-start.25
  318.1 4.2 %collective-permute-done.25 = f32[3,1,256]{2,1,0:T(1,128)S(1)} collective-permute-done((f32[3,1,256]{2,1,0:T(1,128)S(1)}, f32[3,1,256]{2,1,0:T(1,128)S(1)}, u32[]{:S(2)}, u32[]{:S(2)}) %collective-permute-start.25) | collective-permute-done | bytes 3104 | tf_op jit(solution)/shard_map/ppermute | solution.py:28
  322.4 3.4 collective-permute-start.26
  325.8 1.3 collective-permute-start.27
  327.1 2.7 collective-permute-done.27
  330.3 0.8 broadcast_select_fusion.2
  331.2 2.8 collective-permute-start.28
  334.1 1.3 collective-permute-start.29
  335.4 4.2 %collective-permute-done.29 = f32[3,1,256]{2,1,0:T(1,128)S(1)} collective-permute-done((f32[3,1,256]{2,1,0:T(1,128)S(1)}, f32[3,1,256]{2,1,0:T(1,128)S(1)}, u32[]{:S(2)}, u32[]{:S(2)}) %collective-permute-start.29) | collective-permute-done | bytes 3104 | tf_op jit(solution)/shard_map/ppermute | solution.py:28
  339.7 3.4 collective-permute-start.30
  343.1 1.3 collective-permute-start.31
  344.4 2.7 collective-permute-done.31
  347.6 0.8 broadcast_select_fusion.1
  348.5 2.8 collective-permute-start.32
  351.4 1.3 collective-permute-start.33
  352.7 4.2 %collective-permute-done.33 = f32[3,1,256]{2,1,0:T(1,128)S(1)} collective-permute-done((f32[3,1,256]{2,1,0:T(1,128)S(1)}, f32[3,1,256]{2,1,0:T(1,128)S(1)}, u32[]{:S(2)}, u32[]{:S(2)}) %collective-permute-start.33) | collective-permute-done | bytes 3104 | tf_op jit(solution)/shard_map/ppermute | solution.py:28
  356.9 3.4 collective-permute-start.34
  360.3 1.3 collective-permute-start.35
  361.6 2.7 collective-permute-done.35
  364.9 0.8 broadcast_select_fusion
  (150 shorter events, 13.7 us)
Async XLA Ops:
  7.2 1.2 copy-start
  7.2 1.2 copy-start.1
  7.2 268.8 %all-reduce.3.cloned.1.call-start = ((), (), s32[]{:S(2)}) async-start(), calls=%async_computation | async-start | bytes 196608 | tf_op jit(solution)/shard_map/psum | solution.py:134
  8.4 6.2 %copy-start.6 = (f32[11]{0:T(128)S(1)}, f32[11]{0:T(128)}, u32[]{:S(2)}) copy-start(f32[11]{0:T(128)} %param.18) | copy-start | bytes 136
  8.4 6.9 %copy-start.9 = (s32[32,256]{1,0:T(8,128)S(1)}, s32[32,256]{1,0:T(8,128)}, u32[]{:S(2)}) copy-start(s32[32,256]{1,0:T(8,128)} %param.17) | copy-start | bytes 98308
  8.4 67.9 %collective-permute-start = (f32[4,1,256]{2,1,0:T(1,128)S(1)}, f32[4,1,256]{2,1,0:T(1,128)S(1)}, u32[]{:S(2)}, u32[]{:S(2)}) collective-permute-start(f32[4,1,256]{2,1,0:T(1,128)S(1)} %get-tuple-element.32), channel_id=1, source_target_pairs={{0,8},{8,16},{16,24},{1,9},{9,17},{17,25},{2,10},{10,18},{18,26},{... | collective-permute-start | bytes 12296 | tf_op jit(solution)/shard_map/ppermute | solution.py:25
  13.3 63.0 %collective-permute-start.1 = (f32[4,1,256]{2,1,0:T(1,128)S(1)}, f32[4,1,256]{2,1,0:T(1,128)S(1)}, u32[]{:S(2)}, u32[]{:S(2)}) collective-permute-start(f32[4,1,256]{2,1,0:T(1,128)S(1)} %get-tuple-element.33), channel_id=1, source_target_pairs={{8,0},{16,8},{24,16},{9,1},{17,9},{25,17},{10,2},{18,10},{26,18},{... | collective-permute-start | bytes 12296 | tf_op jit(solution)/shard_map/ppermute | solution.py:28
  15.3 7.0 %copy-start.4 = (f32[32,256]{1,0:T(8,128)S(1)}, f32[32,256]{1,0:T(8,128)}, u32[]{:S(2)}) copy-start(f32[32,256]{1,0:T(8,128)} %param.14) | copy-start | bytes 98308
  22.3 5.9 %copy-start.7 = (f32[32,256]{1,0:T(8,128)S(1)}, f32[32,256]{1,0:T(8,128)}, u32[]{:S(2)}) copy-start(f32[32,256]{1,0:T(8,128)} %param.15) | copy-start | bytes 98308
  22.3 5.9 %copy-start.8 = (s32[32,256]{1,0:T(8,128)S(1)}, s32[32,256]{1,0:T(8,128)}, u32[]{:S(2)}) copy-start(s32[32,256]{1,0:T(8,128)} %param.16) | copy-start | bytes 98308
  22.3 35.3 %collective-permute-start.12 = (f32[2,1,256]{2,1,0:T(1,128)S(1)}, f32[2,1,256]{2,1,0:T(1,128)S(1)}, u32[]{:S(2)}, u32[]{:S(2)}) collective-permute-start(f32[2,1,256]{2,1,0:T(1,128)S(1)} %get-tuple-element.82), channel_id=1, source_target_pairs={{0,8},{8,16},{16,24},{1,9},{9,17},{17,25},{2,10},{10,18},{18,26},{... | collective-permute-start | bytes 6152 | tf_op jit(solution)/shard_map/ppermute | solution.py:25
  26.9 30.8 %collective-permute-start.13 = (f32[2,1,256]{2,1,0:T(1,128)S(1)}, f32[2,1,256]{2,1,0:T(1,128)S(1)}, u32[]{:S(2)}, u32[]{:S(2)}) collective-permute-start(f32[2,1,256]{2,1,0:T(1,128)S(1)} %get-tuple-element.83), channel_id=1, source_target_pairs={{8,0},{16,8},{24,16},{9,1},{17,9},{25,17},{10,2},{18,10},{26,18},{... | collective-permute-start | bytes 6152 | tf_op jit(solution)/shard_map/ppermute | solution.py:28
  28.2 35.9 %collective-permute-start.8 = (f32[3,1,256]{2,1,0:T(1,128)S(1)}, f32[3,1,256]{2,1,0:T(1,128)S(1)}, u32[]{:S(2)}, u32[]{:S(2)}) collective-permute-start(f32[3,1,256]{2,1,0:T(1,128)S(1)} %get-tuple-element.108), channel_id=1, source_target_pairs={{0,8},{8,16},{16,24},{1,9},{9,17},{17,25},{2,10},{10,18},{18,26},{... | collective-permute-start | bytes 9224 | tf_op jit(solution)/shard_map/ppermute | solution.py:25
  33.2 0.7 copy-start.10
  57.8 2.6 collective-permute-start.14
  59.1 4.9 %collective-permute-start.15 = (f32[2,34,1]{2,1,0:T(8,128)S(1)}, f32[2,34,1]{2,1,0:T(8,128)S(1)}, u32[]{:S(2)}, u32[]{:S(2)}) collective-permute-start(f32[2,34,1]{2,1,0:T(8,128)S(1)} %get-tuple-element.81), channel_id=1, source_target_pairs={{1,0},{2,1},{3,2},{4,3},{5,4},{6,5},{7,6},{9,8},{10,9},{11,10},{12... | collective-permute-start | bytes 824 | tf_op jit(solution)/shard_map/ppermute | solution.py:28
  60.4 6.4 %collective-permute-start.9 = (f32[3,1,256]{2,1,0:T(1,128)S(1)}, f32[3,1,256]{2,1,0:T(1,128)S(1)}, u32[]{:S(2)}, u32[]{:S(2)}) collective-permute-start(f32[3,1,256]{2,1,0:T(1,128)S(1)} %get-tuple-element.109), channel_id=1, source_target_pairs={{8,0},{16,8},{24,16},{9,1},{17,9},{25,17},{10,2},{18,10},{26,18},{... | collective-permute-start | bytes 9224 | tf_op jit(solution)/shard_map/ppermute | solution.py:28
  66.9 5.3 %collective-permute-start.10 = (f32[3,34,1]{2,1,0:T(8,128)S(1)}, f32[3,34,1]{2,1,0:T(8,128)S(1)}, u32[]{:S(2)}, u32[]{:S(2)}) collective-permute-start(f32[3,34,1]{2,1,0:T(8,128)S(1)} %get-tuple-element.68), channel_id=1, source_target_pairs={{0,1},{1,2},{2,3},{3,4},{4,5},{5,6},{6,7},{8,9},{9,10},{10,11},{11... | collective-permute-start | bytes 1232 | tf_op jit(solution)/shard_map/ppermute | solution.py:25
  70.8 5.2 %collective-permute-start.11 = (f32[3,34,1]{2,1,0:T(8,128)S(1)}, f32[3,34,1]{2,1,0:T(8,128)S(1)}, u32[]{:S(2)}, u32[]{:S(2)}) collective-permute-start(f32[3,34,1]{2,1,0:T(8,128)S(1)} %get-tuple-element.69), channel_id=1, source_target_pairs={{1,0},{2,1},{3,2},{4,3},{5,4},{6,5},{7,6},{9,8},{10,9},{11,10},{12... | collective-permute-start | bytes 1232 | tf_op jit(solution)/shard_map/ppermute | solution.py:28
  76.5 6.1 %collective-permute-start.2 = (f32[4,130,1]{2,1,0:T(8,128)S(1)}, f32[4,130,1]{2,1,0:T(8,128)S(1)}, u32[]{:S(2)}, u32[]{:S(2)}) collective-permute-start(f32[4,130,1]{2,1,0:T(8,128)S(1)} %get-tuple-element.28), channel_id=1, source_target_pairs={{0,1},{1,2},{2,3},{3,4},{4,5},{5,6},{6,7},{8,9},{9,10},{10,11},{11... | collective-permute-start | bytes 6248 | tf_op jit(solution)/shard_map/ppermute | solution.py:25
  81.3 3.5 collective-permute-start.3
  85.4 0.9 copy-start.2
  86.5 6.3 %collective-permute-start.4 = (f32[4,1,256]{2,1,0:T(1,128)S(1)}, f32[4,1,256]{2,1,0:T(1,128)S(1)}, u32[]{:S(2)}, u32[]{:S(2)}) collective-permute-start(f32[4,1,256]{2,1,0:T(1,128)S(1)} %get-tuple-element.30), channel_id=1, source_target_pairs={{0,8},{8,16},{16,24},{1,9},{9,17},{17,25},{2,10},{10,18},{18,26},{... | collective-permute-start | bytes 12296 | tf_op jit(solution)/shard_map/ppermute | solution.py:25
  91.4 5.5 %collective-permute-start.5 = (f32[4,1,256]{2,1,0:T(1,128)S(1)}, f32[4,1,256]{2,1,0:T(1,128)S(1)}, u32[]{:S(2)}, u32[]{:S(2)}) collective-permute-start(f32[4,1,256]{2,1,0:T(1,128)S(1)} %get-tuple-element.31), channel_id=1, source_target_pairs={{8,0},{16,8},{24,16},{9,1},{17,9},{25,17},{10,2},{18,10},{26,18},{... | collective-permute-start | bytes 12296 | tf_op jit(solution)/shard_map/ppermute | solution.py:28
  97.1 30.1 %collective-permute-start.6 = (f32[4,130,1]{2,1,0:T(8,128)S(1)}, f32[4,130,1]{2,1,0:T(8,128)S(1)}, u32[]{:S(2)}, u32[]{:S(2)}) collective-permute-start(f32[4,130,1]{2,1,0:T(8,128)S(1)} %get-tuple-element.26), channel_id=1, source_target_pairs={{0,1},{1,2},{2,3},{3,4},{4,5},{5,6},{6,7},{8,9},{9,10},{10,11},{11... | collective-permute-start | bytes 6248 | tf_op jit(solution)/shard_map/ppermute | solution.py:25
  102.0 25.2 %collective-permute-start.7 = (f32[4,130,1]{2,1,0:T(8,128)S(1)}, f32[4,130,1]{2,1,0:T(8,128)S(1)}, u32[]{:S(2)}, u32[]{:S(2)}) collective-permute-start(f32[4,130,1]{2,1,0:T(8,128)S(1)} %get-tuple-element.27), channel_id=1, source_target_pairs={{1,0},{2,1},{3,2},{4,3},{5,4},{6,5},{7,6},{9,8},{10,9},{11,10},{12... | collective-permute-start | bytes 6248 | tf_op jit(solution)/shard_map/ppermute | solution.py:28
  128.3 0.7 copy-start.3
  152.9 0.6 copy-start.5
  276.9 4.7 %collective-permute-start.16 = (f32[3,1,256]{2,1,0:T(1,128)S(1)}, f32[3,1,256]{2,1,0:T(1,128)S(1)}, u32[]{:S(2)}, u32[]{:S(2)}) collective-permute-start(f32[3,1,256]{2,1,0:T(1,128)S(1)} %get-tuple-element.78), channel_id=1, source_target_pairs={{0,8},{8,16},{16,24},{1,9},{9,17},{17,25},{2,10},{10,18},{18,26},{... | collective-permute-start | bytes 9224 | tf_op jit(solution)/shard_map/ppermute | solution.py:25
  280.3 5.5 %collective-permute-start.17 = (f32[3,1,256]{2,1,0:T(1,128)S(1)}, f32[3,1,256]{2,1,0:T(1,128)S(1)}, u32[]{:S(2)}, u32[]{:S(2)}) collective-permute-start(f32[3,1,256]{2,1,0:T(1,128)S(1)} %get-tuple-element.79), channel_id=1, source_target_pairs={{8,0},{16,8},{24,16},{9,1},{17,9},{25,17},{10,2},{18,10},{26,18},{... | collective-permute-start | bytes 9224 | tf_op jit(solution)/shard_map/ppermute | solution.py:28
  285.9 2.6 collective-permute-start.18
  287.2 6.6 %collective-permute-start.19 = (f32[3,34,1]{2,1,0:T(8,128)S(1)}, f32[3,34,1]{2,1,0:T(8,128)S(1)}, u32[]{:S(2)}, u32[]{:S(2)}) collective-permute-start(f32[3,34,1]{2,1,0:T(8,128)S(1)} %get-tuple-element.65), channel_id=1, source_target_pairs={{1,0},{2,1},{3,2},{4,3},{5,4},{6,5},{7,6},{9,8},{10,9},{11,10},{12... | collective-permute-start | bytes 1232 | tf_op jit(solution)/shard_map/ppermute | solution.py:28
  295.2 5.6 %collective-permute-start.20 = (f32[3,1,256]{2,1,0:T(1,128)S(1)}, f32[3,1,256]{2,1,0:T(1,128)S(1)}, u32[]{:S(2)}, u32[]{:S(2)}) collective-permute-start(f32[3,1,256]{2,1,0:T(1,128)S(1)} %get-tuple-element.76), channel_id=1, source_target_pairs={{0,8},{8,16},{16,24},{1,9},{9,17},{17,25},{2,10},{10,18},{18,26},{... | collective-permute-start | bytes 9224 | tf_op jit(solution)/shard_map/ppermute | solution.py:25
  299.5 5.5 %collective-permute-start.21 = (f32[3,1,256]{2,1,0:T(1,128)S(1)}, f32[3,1,256]{2,1,0:T(1,128)S(1)}, u32[]{:S(2)}, u32[]{:S(2)}) collective-permute-start(f32[3,1,256]{2,1,0:T(1,128)S(1)} %get-tuple-element.77), channel_id=1, source_target_pairs={{8,0},{16,8},{24,16},{9,1},{17,9},{25,17},{10,2},{18,10},{26,18},{... | collective-permute-start | bytes 9224 | tf_op jit(solution)/shard_map/ppermute | solution.py:28
  305.1 4.7 %collective-permute-start.22 = (f32[3,34,1]{2,1,0:T(8,128)S(1)}, f32[3,34,1]{2,1,0:T(8,128)S(1)}, u32[]{:S(2)}, u32[]{:S(2)}) collective-permute-start(f32[3,34,1]{2,1,0:T(8,128)S(1)} %get-tuple-element.62), channel_id=1, source_target_pairs={{0,1},{1,2},{2,3},{3,4},{4,5},{5,6},{6,7},{8,9},{9,10},{10,11},{11... | collective-permute-start | bytes 1232 | tf_op jit(solution)/shard_map/ppermute | solution.py:25
  308.5 4.0 %collective-permute-start.23 = (f32[3,34,1]{2,1,0:T(8,128)S(1)}, f32[3,34,1]{2,1,0:T(8,128)S(1)}, u32[]{:S(2)}, u32[]{:S(2)}) collective-permute-start(f32[3,34,1]{2,1,0:T(8,128)S(1)} %get-tuple-element.63), channel_id=1, source_target_pairs={{1,0},{2,1},{3,2},{4,3},{5,4},{6,5},{7,6},{9,8},{10,9},{11,10},{12... | collective-permute-start | bytes 1232 | tf_op jit(solution)/shard_map/ppermute | solution.py:28
  314.0 4.1 %collective-permute-start.24 = (f32[3,1,256]{2,1,0:T(1,128)S(1)}, f32[3,1,256]{2,1,0:T(1,128)S(1)}, u32[]{:S(2)}, u32[]{:S(2)}) collective-permute-start(f32[3,1,256]{2,1,0:T(1,128)S(1)} %get-tuple-element.74), channel_id=1, source_target_pairs={{0,8},{8,16},{16,24},{1,9},{9,17},{17,25},{2,10},{10,18},{18,26},{... | collective-permute-start | bytes 9224 | tf_op jit(solution)/shard_map/ppermute | solution.py:25
  316.8 5.5 %collective-permute-start.25 = (f32[3,1,256]{2,1,0:T(1,128)S(1)}, f32[3,1,256]{2,1,0:T(1,128)S(1)}, u32[]{:S(2)}, u32[]{:S(2)}) collective-permute-start(f32[3,1,256]{2,1,0:T(1,128)S(1)} %get-tuple-element.75), channel_id=1, source_target_pairs={{8,0},{16,8},{24,16},{9,1},{17,9},{25,17},{10,2},{18,10},{26,18},{... | collective-permute-start | bytes 9224 | tf_op jit(solution)/shard_map/ppermute | solution.py:28
  322.4 4.7 %collective-permute-start.26 = (f32[3,34,1]{2,1,0:T(8,128)S(1)}, f32[3,34,1]{2,1,0:T(8,128)S(1)}, u32[]{:S(2)}, u32[]{:S(2)}) collective-permute-start(f32[3,34,1]{2,1,0:T(8,128)S(1)} %get-tuple-element.60), channel_id=1, source_target_pairs={{0,1},{1,2},{2,3},{3,4},{4,5},{5,6},{6,7},{8,9},{9,10},{10,11},{11... | collective-permute-start | bytes 1232 | tf_op jit(solution)/shard_map/ppermute | solution.py:25
  325.8 4.0 %collective-permute-start.27 = (f32[3,34,1]{2,1,0:T(8,128)S(1)}, f32[3,34,1]{2,1,0:T(8,128)S(1)}, u32[]{:S(2)}, u32[]{:S(2)}) collective-permute-start(f32[3,34,1]{2,1,0:T(8,128)S(1)} %get-tuple-element.61), channel_id=1, source_target_pairs={{1,0},{2,1},{3,2},{4,3},{5,4},{6,5},{7,6},{9,8},{10,9},{11,10},{12... | collective-permute-start | bytes 1232 | tf_op jit(solution)/shard_map/ppermute | solution.py:28
  331.2 4.1 %collective-permute-start.28 = (f32[3,1,256]{2,1,0:T(1,128)S(1)}, f32[3,1,256]{2,1,0:T(1,128)S(1)}, u32[]{:S(2)}, u32[]{:S(2)}) collective-permute-start(f32[3,1,256]{2,1,0:T(1,128)S(1)} %get-tuple-element.72), channel_id=1, source_target_pairs={{0,8},{8,16},{16,24},{1,9},{9,17},{17,25},{2,10},{10,18},{18,26},{... | collective-permute-start | bytes 9224 | tf_op jit(solution)/shard_map/ppermute | solution.py:25
  334.1 5.5 %collective-permute-start.29 = (f32[3,1,256]{2,1,0:T(1,128)S(1)}, f32[3,1,256]{2,1,0:T(1,128)S(1)}, u32[]{:S(2)}, u32[]{:S(2)}) collective-permute-start(f32[3,1,256]{2,1,0:T(1,128)S(1)} %get-tuple-element.73), channel_id=1, source_target_pairs={{8,0},{16,8},{24,16},{9,1},{17,9},{25,17},{10,2},{18,10},{26,18},{... | collective-permute-start | bytes 9224 | tf_op jit(solution)/shard_map/ppermute | solution.py:28
  339.7 4.7 %collective-permute-start.30 = (f32[3,34,1]{2,1,0:T(8,128)S(1)}, f32[3,34,1]{2,1,0:T(8,128)S(1)}, u32[]{:S(2)}, u32[]{:S(2)}) collective-permute-start(f32[3,34,1]{2,1,0:T(8,128)S(1)} %get-tuple-element.58), channel_id=1, source_target_pairs={{0,1},{1,2},{2,3},{3,4},{4,5},{5,6},{6,7},{8,9},{9,10},{10,11},{11... | collective-permute-start | bytes 1232 | tf_op jit(solution)/shard_map/ppermute | solution.py:25
  343.1 4.0 %collective-permute-start.31 = (f32[3,34,1]{2,1,0:T(8,128)S(1)}, f32[3,34,1]{2,1,0:T(8,128)S(1)}, u32[]{:S(2)}, u32[]{:S(2)}) collective-permute-start(f32[3,34,1]{2,1,0:T(8,128)S(1)} %get-tuple-element.59), channel_id=1, source_target_pairs={{1,0},{2,1},{3,2},{4,3},{5,4},{6,5},{7,6},{9,8},{10,9},{11,10},{12... | collective-permute-start | bytes 1232 | tf_op jit(solution)/shard_map/ppermute | solution.py:28
  348.5 4.1 %collective-permute-start.32 = (f32[3,1,256]{2,1,0:T(1,128)S(1)}, f32[3,1,256]{2,1,0:T(1,128)S(1)}, u32[]{:S(2)}, u32[]{:S(2)}) collective-permute-start(f32[3,1,256]{2,1,0:T(1,128)S(1)} %get-tuple-element.70), channel_id=1, source_target_pairs={{0,8},{8,16},{16,24},{1,9},{9,17},{17,25},{2,10},{10,18},{18,26},{... | collective-permute-start | bytes 9224 | tf_op jit(solution)/shard_map/ppermute | solution.py:25
  351.4 5.5 %collective-permute-start.33 = (f32[3,1,256]{2,1,0:T(1,128)S(1)}, f32[3,1,256]{2,1,0:T(1,128)S(1)}, u32[]{:S(2)}, u32[]{:S(2)}) collective-permute-start(f32[3,1,256]{2,1,0:T(1,128)S(1)} %get-tuple-element.71), channel_id=1, source_target_pairs={{8,0},{16,8},{24,16},{9,1},{17,9},{25,17},{10,2},{18,10},{26,18},{... | collective-permute-start | bytes 9224 | tf_op jit(solution)/shard_map/ppermute | solution.py:28
  356.9 4.7 %collective-permute-start.34 = (f32[3,34,1]{2,1,0:T(8,128)S(1)}, f32[3,34,1]{2,1,0:T(8,128)S(1)}, u32[]{:S(2)}, u32[]{:S(2)}) collective-permute-start(f32[3,34,1]{2,1,0:T(8,128)S(1)} %get-tuple-element.56), channel_id=1, source_target_pairs={{0,1},{1,2},{2,3},{3,4},{4,5},{5,6},{6,7},{8,9},{9,10},{10,11},{11... | collective-permute-start | bytes 1232 | tf_op jit(solution)/shard_map/ppermute | solution.py:25
  360.3 4.1 %collective-permute-start.35 = (f32[3,34,1]{2,1,0:T(8,128)S(1)}, f32[3,34,1]{2,1,0:T(8,128)S(1)}, u32[]{:S(2)}, u32[]{:S(2)}) collective-permute-start(f32[3,34,1]{2,1,0:T(8,128)S(1)} %get-tuple-element.57), channel_id=1, source_target_pairs={{1,0},{2,1},{3,2},{4,3},{5,4},{6,5},{7,6},{9,8},{10,9},{11,10},{12... | collective-permute-start | bytes 1232 | tf_op jit(solution)/shard_map/ppermute | solution.py:28
Sparse Core Ops, SparseCore 0:
  153.7 122.1 all-reduce.2
where the time goes:
time: 378 us; the launch traced here: 374 us
  waiting for transfers between devices  175 us (46%)
  starting transfers between devices  88.4 us (23%)
  local copies, waits for them, and re-layouts  75.5 us (20%)
  other arithmetic  20.3 us (5%)
  between operations  15.2 us (4%)
    psum x1, waiting for transfers between devices, per_device(): summed = lax.psum(per_step, ('rows', 'cols'))  122 us
    ppermute x18, starting transfers between devices, padded_2(): lax.ppermute(lax.slice_in_dim(block, block.shape[dim] - width, None, axis...  65.1 us
    ppermute x18, waiting for transfers between devices, padded_2(): lax.ppermute(lax.slice_in_dim(block, 0, width, axis=dim), axis, backward)  52.1 us
    gather x3, local copies, waits for them, and re-layouts, sample(): jnp.take(velocity.reshape(-1), flat_index) * owned_weight  35.3 us
    gather x3, local copies, waits for them, and re-layouts, sample(): jnp.take(surface.reshape(-1), flat_index) * owned_weight  35.3 us
    ppermute x18, starting transfers between devices, padded_2(): lax.ppermute(lax.slice_in_dim(block, 0, width, axis=dim), axis, backward)  23.3 us
  transfers between devices with their start and end apart: 37, of which 16 were waited for; matrix products, arithmetic and copies ran while one was open for 15% of the time, Pallas kernels for 0%

commit v1 on v0

v1 whole, which is shorter than its diff:
```python
import functools

import jax
import jax.numpy as jnp
from jax import lax
from jax.experimental import pallas as pl
from jax.experimental.pallas import tpu as pltpu
from jax.sharding import PartitionSpec as P

NCLASS = 11
SUB = 3
FSTEPS = 6
RATIO = 18
REACH = 128

gravity = 9.81
coarse_spacing = 90.0
coarse_tick = 0.25
fine_spacing = 5.0
depth_floor = 0.01
dry_depth = 0.05
fine_tick = coarse_tick / SUB

LANES = 128
PAD = 8
MESH = pl.DeviceIdType.MESH


def turn(x, shift, axis):
    return pltpu.roll(x, shift % x.shape[axis], axis)


def coarse_step(surf, depth, rows_flux, cols_flux):
    total = depth + surf

    def face(flux, axis):
        d = jnp.minimum(total, turn(total, -1, axis))
        slope = turn(surf, -1, axis) - surf
        return jnp.minimum(d, 1.0) * (flux - (coarse_tick * gravity / coarse_spacing) * d * slope)

    new_rows = face(rows_flux, 0)
    new_cols = face(cols_flux, 1)
    surf = surf - (coarse_tick / coarse_spacing) * (
        new_rows - turn(new_rows, 1, 0) + (new_cols - turn(new_cols, 1, 1))
    )
    return surf, new_rows, new_cols


def fine_run(water, bed, rough, row_keep, col_keep, top):
    bed_faces = [jnp.maximum(bed, turn(bed, -1, axis)) for axis in (0, 1)]
    drag = []
    for axis in (0, 1):
        n = 0.5 * (rough + turn(rough, -1, axis))
        drag.append((fine_tick * gravity) * n * n)
    keep = (row_keep, col_keep)
    flux = [None, None]
    first_row = lax.broadcasted_iota(jnp.int32, water.shape, 0) == 0
    for step in range(FSTEPS):
        surf = bed + water
        new = []
        for axis in (0, 1):
            after = turn(surf, -1, axis)
            d = jnp.maximum(jnp.maximum(surf, after) - bed_faces[axis], 0.0)
            push = (fine_tick * gravity / fine_spacing) * d * (after - surf)
            wet = jnp.minimum(d * (1.0 / dry_depth), 1.0)
            if step == 0:
                value = wet * (-push)
            else:
                power = jnp.exp((-7.0 / 3.0) * jnp.log(jnp.maximum(d, depth_floor)))
                friction = 1.0 + drag[axis] * jnp.abs(flux[axis]) * power
                value = wet * (flux[axis] - push) / friction
            if keep[axis] is not None:
                value = jnp.where(keep[axis], value, 0.0)
            new.append(value)
        above = turn(new[0], 1, 0)
        if top is not None:
            above = jnp.where(first_row, top(step, water[0:1, :], bed[0:1, :]), above)
        water = water - (fine_tick / fine_spacing) * (new[0] - above + (new[1] - turn(new[1], 1, 1)))
        flux = new
    return water, flux[0], flux[1]


def kernel(
    nrow, ncol, nslots,
    eta_ref, flux_ref, depth_ref, bed_ref, fdepth_ref, wet_ref, class_ref, manning_ref, nest_ref,
    out_eta, out_water, out_flux,
    ce, cs, pc, cl, cr, fe, pf, fl, fr, samp, sbuf, rbuf, acc,
    send_sem, recv_sem, ssend_sem, srecv_sem,
):
    r = lax.axis_index("rows")
    c = lax.axis_index("cols")
    th, tw = eta_ref.shape
    fh = bed_ref.shape[0]
    nb = nest_ref.shape[0]
    width = tw * ncol
    up, dn = r > 0, r < nrow - 1
    lf, rt = c > 0, c < ncol - 1
    around = [
        (up, r - 1, c), (dn, r + 1, c), (lf, r, c - 1), (rt, r, c + 1),
        (up & lf, r - 1, c - 1), (up & rt, r - 1, c + 1),
        (dn & lf, r + 1, c - 1), (dn & rt, r + 1, c + 1),
    ]
    arrives = [dn, up, rt, lf, dn & rt, dn & lf, up & rt, up & lf]

    barrier = pltpu.get_barrier_semaphore()
    expected = jnp.int32(0)
    for there, rr, cc in around:
        @pl.when(there)
        def _(rr=rr, cc=cc):
            pl.semaphore_signal(barrier, inc=1, device_id=(rr, cc), device_id_type=MESH)
        expected = expected + there.astype(jnp.int32)

    @pl.when(r == 0)
    def _():
        for k in range(3):
            for rr in range(nrow):
                if k == 0 and rr == 0:
                    continue

                @pl.when(c + k < ncol)
                def _(k=k, rr=rr):
                    pl.semaphore_signal(barrier, inc=1, device_id=(rr, c + k), device_id_type=MESH)

    for k in range(3):
        sends = c - k >= 0
        if k == 0:
            sends = r > 0
        expected = expected + sends.astype(jnp.int32)

    def copies(ext, packed, left, right, high, base):
        a, b = PAD, PAD + high
        whole = [
            (ext.at[:, a:a + PAD, 0:tw], ext.at[:, b:b + PAD, 0:tw]),
            (ext.at[:, b - PAD:b, 0:tw], ext.at[:, 0:a, 0:tw]),
            (packed, right.at[a:b]),
            (packed, left.at[a:b]),
            (packed.at[0:PAD], right.at[b:b + PAD]),
            (packed.at[0:PAD], left.at[b:b + PAD]),
            (packed.at[high - PAD:high], right.at[0:PAD]),
            (packed.at[high - PAD:high], left.at[0:PAD]),
        ]
        return [
            functools.partial(
                pltpu.make_async_remote_copy, src_ref=src, dst_ref=dst,
                send_sem=send_sem.at[base + d], recv_sem=recv_sem.at[base + d],
                device_id=(around[d][1], around[d][2]), device_id_type=MESH,
            )
            for d, (src, dst) in enumerate(whole)
        ]

    coarse_copies = copies(ce, pc, cl, cr, th, 0)
    fine_copies = copies(fe, pf, fl, fr, fh, 8)

    def start(made):
        for d in (2, 3, 0, 1, 4, 5, 6, 7):
            @pl.when(around[d][0])
            def _(d=d):
                made[d]().start()

    def wait_in(made):
        for d in range(8):
            @pl.when(arrives[d])
            def _(d=d):
                made[d]().wait_recv()

    def wait_out(made):
        for d in range(8):
            @pl.when(around[d][0])
            def _(d=d):
                made[d]().wait_send()

    def blank(ext, left, right, high):
        a, b = PAD, PAD + high
        fields = ext.shape[0]

        @pl.when(jnp.logical_not(up))
        def _():
            ext[:, 0:a, 0:tw] = jnp.zeros((fields, PAD, tw), jnp.float32)
            left[0:a, :] = jnp.zeros((PAD, LANES), jnp.float32)
            right[0:a, :] = jnp.zeros((PAD, LANES), jnp.float32)

        @pl.when(jnp.logical_not(dn))
        def _():
            ext[:, b:b + PAD, 0:tw] = jnp.zeros((fields, PAD, tw), jnp.float32)
            left[b:b + PAD, :] = jnp.zeros((PAD, LANES), jnp.float32)
            right[b:b + PAD, :] = jnp.zeros((PAD, LANES), jnp.float32)

        @pl.when(jnp.logical_not(lf))
        def _():
            left[...] = jnp.zeros(left.shape, jnp.float32)

        @pl.when(jnp.logical_not(rt))
        def _():
            right[...] = jnp.zeros(right.shape, jnp.float32)

    def pack(fields, reach):
        high = fields[0].shape[0]
        lane = lax.broadcasted_iota(jnp.int32, (high, LANES), 1)
        out = None
        for q, field in enumerate(fields):
            edge = jnp.where(lane < LANES // 2, field[:, 0:LANES], field[:, tw - LANES:tw])
            if q == 0:
                out = edge
            else:
                lo = 2 * reach * q - reach
                out = jnp.where((lane >= lo) & (lane < lo + 2 * reach), turn(edge, 2 * reach * q, 1), out)
        return out

    def unpack(ext, left, right, reach):
        lane = lax.broadcasted_iota(jnp.int32, left.shape, 1)
        of_right = lane < reach
        for q in range(1, ext.shape[0]):
            of_right = of_right | ((lane >= 2 * reach * q) & (lane < 2 * reach * q + reach))
        merged = jnp.where(of_right, right[...], left[...])
        for q in range(ext.shape[0]):
            ext[q, :, tw:tw + LANES] = merged if q == 0 else turn(merged, -2 * reach * q, 1)

    eta, depth = eta_ref[...], depth_ref[...]
    f0, f1 = flux_ref[0], flux_ref[1]
    for q, field in enumerate((eta, depth, f0, f1)):
        ce[q, PAD:PAD + th, 0:tw] = field
    pc[...] = pack((eta, depth, f0, f1), 2)
    blank(ce, cl, cr, th)
    pl.semaphore_wait(barrier, expected)
    start(coarse_copies)

    kind = class_ref[...]
    rough = jnp.zeros(kind.shape, jnp.float32)
    for i in range(NCLASS):
        rough = jnp.where(kind == i, manning_ref[i], rough)
    water = wet_ref[...].astype(jnp.float32) * fdepth_ref[...]
    bed = bed_ref[...]
    for q, field in enumerate((water, bed, rough)):
        fe[q, PAD:PAD + fh, 0:tw] = field
    pf[...] = pack((water, bed, rough), FSTEPS)
    blank(fe, fl, fr, fh)
    start(fine_copies)

    wait_in(coarse_copies)
    unpack(ce, cl, cr, 2)
    s, d, fa, fb = ce[0], ce[1], ce[2], ce[3]
    s, fa, fb = coarse_step(s, d, fa, fb)
    cs[0] = s[PAD:PAD + th, 0:tw]
    cs[1] = fa[PAD:PAD + th, 0:tw]
    s, fa, fb = coarse_step(s, d, fa, fb)
    cs[2] = s[PAD:PAD + th, 0:tw]
    cs[3] = fa[PAD:PAD + th, 0:tw]
    out_eta[...] = s[PAD:PAD + th, 0:tw]

    low = (jnp.maximum(c * tw - (tw + REACH) + RATIO - 1, 0)) // RATIO
    seg0 = low + lax.rem(r + nrow - lax.rem(low, nrow), nrow)
    lane_t = lax.broadcasted_iota(jnp.int32, (8, tw), 1)
    values = []
    for slot in range(nslots):
        seg = seg0 + slot * nrow
        cell = nest_ref[jnp.minimum(seg * RATIO, nb - 1)]
        row = cell // width
        col = cell - row * width - c * tw
        row = row - r * th
        held = (row >= 0) & (row < th)
        row = jnp.clip(row, 0, th - 1)
        col = jnp.where(held, col, -1)
        o = slot * 8
        samp[o:o + 1, :] = ce[0, pl.ds(PAD + row, 1), 0:tw]
        samp[o + 1:o + 2, :] = cs[0, pl.ds(row, 1), :]
        samp[o + 2:o + 3, :] = cs[2, pl.ds(row, 1), :]
        samp[o + 3:o + 4, :] = ce[2, pl.ds(PAD + row, 1), 0:tw]
        samp[o + 4:o + 5, :] = cs[1, pl.ds(row, 1), :]
        samp[o + 5:o + 6, :] = cs[3, pl.ds(row, 1), :]
        samp[o + 6:o + 7, :] = ce[1, pl.ds(PAD + row, 1), 0:tw]
        samp[o + 7:o + 8, :] = jnp.zeros((1, tw), jnp.float32)
        got = jnp.where(lane_t == col, samp[o:o + 8, :], 0.0)
        values.append(jnp.sum(got, axis=1, keepdims=True))
    ext_w = tw + LANES
    lane_e = lax.broadcasted_iota(jnp.int32, (8, ext_w), 1)
    place = jnp.where(lane_e < tw + LANES // 2, lane_e, lane_e - ext_w)

    def sample_copy(k):
        return pltpu.make_async_remote_copy(
            src_ref=sbuf.at[k], dst_ref=rbuf.at[k * nrow + r],
            send_sem=ssend_sem.at[k], recv_sem=srecv_sem.at[k * nrow + r],
            device_id=(0, c - k), device_id_type=MESH,
        )

    for k in range(3):
        at = place + (c - k) * tw
        window = jnp.zeros((8, ext_w), jnp.float32)
        for slot in range(nslots):
            begin = (seg0 + slot * nrow) * RATIO
            window = jnp.where((at >= begin) & (at < begin + RATIO), values[slot], window)
        sbuf[k] = window
        sends = (r > 0) if k == 0 else (c - k >= 0)

        @pl.when(sends)
        def _(k=k):
            sample_copy(k).start()

    wait_in(fine_copies)
    unpack(fe, fl, fr, FSTEPS)

    def keeps(high, first):
        row = lax.broadcasted_iota(jnp.int32, (high, ext_w), 0) + first
        lane = lax.broadcasted_iota(jnp.int32, (high, ext_w), 1)
        col = jnp.where(lane < tw + LANES // 2, lane, lane - ext_w) + c * tw
        return row != fh * nrow - 1, (col != -1) & (col != width - 1)

    row_keep, col_keep = keeps(fh + 2 * PAD, r * fh - PAD)
    w, g0, g1 = fine_run(fe[0], fe[1], fe[2], row_keep, col_keep, None)
    out_water[...] = w[PAD:PAD + fh, 0:tw]
    out_flux[0] = g0[PAD:PAD + fh, 0:tw]
    out_flux[1] = g1[PAD:PAD + fh, 0:tw]

    @pl.when(r == 0)
    def _():
        acc[...] = sbuf[0]
        for k in range(3):
            for rr in range(nrow):
                if k == 0 and rr == 0:
                    continue

                @pl.when(c + k < ncol)
                def _(k=k, rr=rr):
                    j = k * nrow + rr
                    pltpu.make_async_remote_copy(
                        src_ref=sbuf.at[k], dst_ref=rbuf.at[j],
                        send_sem=ssend_sem.at[k], recv_sem=srecv_sem.at[j],
                        device_id=(rr, c + k), device_id_type=MESH,
                    ).wait_recv()
                    acc[...] += rbuf[j]
        level_s = [acc[i:i + 1, :] for i in range(3)]
        still = acc[6:7, :]
        level_v = []
        for i in range(3):
            total = still + level_s[i]
            level_v.append(acc[3 + i:4 + i, :] / jnp.where(total == 0.0, 1.0, total))

        def top(step, w0, b0):
            k = step // SUB
            weight = (step % SUB + 1) / SUB
            bs = (1.0 - weight) * level_s[k] + weight * level_s[k + 1]
            bv = (1.0 - weight) * level_v[k] + weight * level_v[k + 1]
            return w0 * bv + jnp.sqrt(gravity * jnp.maximum(w0, depth_floor)) * (bs - (b0 + w0))

        strip = 2 * PAD
        _, ck = keeps(strip, 0)
        w, g0, g1 = fine_run(
            fe[0, PAD:PAD + strip, :], fe[1, PAD:PAD + strip, :], fe[2, PAD:PAD + strip, :],
            None, ck, top,
        )
        out_water[0:PAD, :] = w[0:PAD, 0:tw]
        out_flux[0, 0:PAD, :] = g0[0:PAD, 0:tw]
        out_flux[1, 0:PAD, :] = g1[0:PAD, 0:tw]

    wait_out(coarse_copies)
    wait_out(fine_copies)
    for k in range(3):
        sends = (r > 0) if k == 0 else (c - k >= 0)

        @pl.when(sends)
        def _(k=k):
            sample_copy(k).wait_send()


def per_device(nrow, ncol, *args):
    c_eta, c_flux, c_depth, f_bed, f_depth, f_wet, f_class, manning, nest_map = args
    th, tw = c_eta.shape
    fh = f_bed.shape[0]
    ext_w = tw + LANES
    segments = -(-nest_map.shape[0] // RATIO)
    last_low = max((ncol - 1) * tw - (tw + REACH) + RATIO - 1, 0) // RATIO
    span = max((tw + REACH) // RATIO + 1, segments - last_low)
    nslots = -(-span // nrow)
    vmem = pl.BlockSpec(memory_space=pltpu.VMEM)
    smem = pl.BlockSpec(memory_space=pltpu.SMEM)
    f32 = jnp.float32
    return pl.pallas_call(
        functools.partial(kernel, nrow, ncol, nslots),
        out_shape=(
            jax.ShapeDtypeStruct((th, tw), f32),
            jax.ShapeDtypeStruct((fh, tw), f32),
            jax.ShapeDtypeStruct((2, fh, tw), f32),
        ),
        in_specs=[vmem] * 7 + [smem] * 2,
        out_specs=(vmem, vmem, vmem),
        scratch_shapes=[
            pltpu.VMEM((4, th + 2 * PAD, ext_w), f32),
            pltpu.VMEM((4, th, tw), f32),
            pltpu.VMEM((th, LANES), f32),
            pltpu.VMEM((th + 2 * PAD, LANES), f32),
            pltpu.VMEM((th + 2 * PAD, LANES), f32),
            pltpu.VMEM((3, fh + 2 * PAD, ext_w), f32),
            pltpu.VMEM((fh, LANES), f32),
            pltpu.VMEM((fh + 2 * PAD, LANES), f32),
            pltpu.VMEM((fh + 2 * PAD, LANES), f32),
            pltpu.VMEM((nslots * 8, tw), f32),
            pltpu.VMEM((3, 8, ext_w), f32),
            pltpu.VMEM((3 * nrow, 8, ext_w), f32),
            pltpu.VMEM((8, ext_w), f32),
            pltpu.SemaphoreType.DMA((16,)),
            pltpu.SemaphoreType.DMA((16,)),
            pltpu.SemaphoreType.DMA((3,)),
            pltpu.SemaphoreType.DMA((3 * nrow,)),
        ],
        compiler_params=pltpu.CompilerParams(
            collective_id=0, has_side_effects=True, vmem_limit_bytes=32 * 1024 * 1024
        ),
    )(*args)


def solution(mesh):
    in_specs = (
        P("rows", "cols"),
        P(None, "rows", "cols"),
        P("rows", "cols"),
        P("rows", "cols"),
        P("rows", "cols"),
        P("rows", "cols"),
        P("rows", "cols"),
        P(),
        P(),
    )
    out_specs = (P("rows", "cols"), P("rows", "cols"), P(None, "rows", "cols"))
    body = functools.partial(per_device, mesh.shape["rows"], mesh.shape["cols"])
    return jax.shard_map(body, mesh=mesh, in_specs=in_specs, out_specs=out_specs, check_vma=False)
```

time: 378 us -> 25.9 us (0.07)
  waiting for transfers between devices: 175 us -> 0 us
  starting transfers between devices: 88.4 us -> 0 us
  local copies, waits for them, and re-layouts: 75.5 us -> 9.03 us
  other arithmetic: 20.3 us -> 0 us
  Pallas kernels: 0 us -> 15.7 us
  between operations: 15.2 us -> 0.66 us
    psum x1 -> x0, waiting for transfers between devices: 122 us -> none  [per_device(): summed = lax.psum(per_step, ('rows', 'cols'))]
    ppermute x36 -> x0, starting transfers between devices: 88.3 us -> none  [the longest x18 65.1 us: padded_2(): lax.ppermute(lax.slice_in_dim(block, block.shape[dim] - width, None, axis...]
    gather x6 -> x0, local copies, waits for them, and re-layouts: 70.7 us -> none  [the longest x3 35.3 us: sample(): jnp.take(velocity.reshape(-1), flat_index) * owned_weight]
    ppermute x36 -> x0, waiting for transfers between devices: 52.2 us -> none  [the longest x18 52.1 us: padded_2(): lax.ppermute(lax.slice_in_dim(block, 0, width, axis=dim), axis, backward)]
    pallas_call x0 -> x1, Pallas kernels: none -> 15.7 us  [per_device(): pl.pallas_call(functools.partial(kernel, nrow, ncol, nslots), out_shape=(...]
    another operation x11 -> x0, other arithmetic: 8.8 us -> none  [the longest x1 6.96 us: per_device(): jnp.stack([f_bed, roughness])]
    unnamed x28 -> x21, local copies, waits for them, and re-layouts: 2.97 us -> 9.03 us
    select_n x8 -> x0, other arithmetic: 5.02 us -> none  [the longest x6 5.01 us: per_device(): first_face = jnp.where(at_top, top_flux, new_rows[0])]
  transfers between devices with their start and end apart: 37 -> 0, of which waited for: 16 -> 0; matrix products, arithmetic and copies ran while one was open for 15% -> 0% of each run, Pallas kernels for 0% -> 0%
where the time goes in v1:
time: 25.9 us; the launch traced here: 25.4 us
  Pallas kernels  15.7 us (61%)
  local copies, waits for them, and re-layouts  9.03 us (35%)
  between operations  0.66 us (3%)
    pallas_call x1, Pallas kernels, per_device(): pl.pallas_call(functools.partial(kernel, nrow, ncol, nslots), out_shape=(...  15.7 us
    unnamed x21, local copies, waits for them, and re-layouts  9.03 us

profile of v1, /device:TPU:0, one launch (start us, length us, event | category | flops | bytes accessed | tf_op | source)
XLA Modules:
  0.0 25.4 jit_solution(8161795326806350520)
XLA Ops:
  0.6 0.0 copy-start
  0.6 0.9 %copy-done = f32[2,128,256]{2,1,0:T(8,128)S(1)} copy-done((f32[2,128,256]{2,1,0:T(8,128)S(1)}, f32[2,128,256]{2,1,0:T(8,128)}, u32[]{:S(2)}) %copy-start) | copy-done | bytes 262168
  1.6 0.0 copy-start.1
  1.6 0.9 %copy-done.1 = f32[128,256]{1,0:T(8,128)S(1)} copy-done((f32[128,256]{1,0:T(8,128)S(1)}, f32[128,256]{1,0:T(8,128)}, u32[]{:S(2)}) %copy-start.1) | copy-done | bytes 131096
  2.5 0.0 copy-start.2
  2.5 0.9 %copy-done.2 = f32[128,256]{1,0:T(8,128)S(1)} copy-done((f32[128,256]{1,0:T(8,128)S(1)}, f32[128,256]{1,0:T(8,128)}, u32[]{:S(2)}) %copy-start.2) | copy-done | bytes 131096
  3.4 0.0 copy-start.3
  3.4 0.8 %copy-done.3 = f32[32,256]{1,0:T(8,128)S(1)} copy-done((f32[32,256]{1,0:T(8,128)S(1)}, f32[32,256]{1,0:T(8,128)}, u32[]{:S(2)}) %copy-start.3) | copy-done | bytes 32792
  4.2 0.0 copy-start.4
  4.2 0.8 %copy-done.4 = f32[32,256]{1,0:T(8,128)S(1)} copy-done((f32[32,256]{1,0:T(8,128)S(1)}, f32[32,256]{1,0:T(8,128)}, u32[]{:S(2)}) %copy-start.4) | copy-done | bytes 32792
  4.9 0.0 copy-start.5
  4.9 0.8 %copy-done.5 = s32[32,256]{1,0:T(8,128)S(1)} copy-done((s32[32,256]{1,0:T(8,128)S(1)}, s32[32,256]{1,0:T(8,128)}, u32[]{:S(2)}) %copy-start.5) | copy-done | bytes 32792
  5.7 0.0 copy-start.6
  5.7 0.8 %copy-done.6 = s32[32,256]{1,0:T(8,128)S(1)} copy-done((s32[32,256]{1,0:T(8,128)S(1)}, s32[32,256]{1,0:T(8,128)}, u32[]{:S(2)}) %copy-start.6) | copy-done | bytes 32792
  6.4 0.0 copy-start.7
  6.4 0.7 %copy-done.7 = s32[2048]{0:T(1024)S(1)} copy-done((s32[2048]{0:T(1024)S(1)}, s32[2048]{0:T(1024)}, u32[]{:S(2)}) %copy-start.7) | copy-done | bytes 8216
  7.1 0.0 copy-start.8
  7.1 0.7 %copy-done.8 = f32[11]{0:T(128)S(1)} copy-done((f32[11]{0:T(128)S(1)}, f32[11]{0:T(128)}, u32[]{:S(2)}) %copy-start.8) | copy-done | bytes 68
  7.8 15.7 %shard_map.112 = (f32[128,256]{1,0:T(8,128)S(1)}, f32[32,256]{1,0:T(8,128)S(1)}, f32[2,32,256]{2,1,0:T(8,128)S(1)}) custom-call(f32[128,256]{1,0:T(8,128)S(1)} %copy-done.1, f32[2,128,256]{2,1,0:T(8,128)S(1)} %copy-done, f32[128,256]{1,0:T(8,128)S(1)} %copy-done.2, f32[32,256]{1,0:T(8,128)S(1)} %copy-done.3, f32[32,256]{1,0:T(8,128)S(1)} %copy-done.4, ...), custom_call_target="tpu_custom_call" | custom-call | tf_op jit(solution)/shard_map/pallas_call | solution.py:376
  23.5 0.7 %copy.15 = f32[128,256]{1,0:T(8,128)} copy(f32[128,256]{1,0:T(8,128)S(1)} %get-tuple-element.6) | data formatting | bytes 262144
  24.2 0.6 %copy.16 = f32[32,256]{1,0:T(8,128)} copy(f32[32,256]{1,0:T(8,128)S(1)} %get-tuple-element.7) | data formatting | bytes 65536
  24.8 0.6 %copy.17 = f32[2,32,256]{2,1,0:T(8,128)} copy(f32[2,32,256]{2,1,0:T(8,128)S(1)} %get-tuple-element.8) | data formatting | bytes 131072
Async XLA Ops:
  0.6 1.0 %copy-start = (f32[2,128,256]{2,1,0:T(8,128)S(1)}, f32[2,128,256]{2,1,0:T(8,128)}, u32[]{:S(2)}) copy-start(f32[2,128,256]{2,1,0:T(8,128)} %flux_ref.1) | copy-start | bytes 786436
  1.6 0.9 %copy-start.1 = (f32[128,256]{1,0:T(8,128)S(1)}, f32[128,256]{1,0:T(8,128)}, u32[]{:S(2)}) copy-start(f32[128,256]{1,0:T(8,128)} %eta_ref.1) | copy-start | bytes 393220
  2.5 0.9 %copy-start.2 = (f32[128,256]{1,0:T(8,128)S(1)}, f32[128,256]{1,0:T(8,128)}, u32[]{:S(2)}) copy-start(f32[128,256]{1,0:T(8,128)} %depth_ref.1) | copy-start | bytes 393220
  3.4 0.8 %copy-start.3 = (f32[32,256]{1,0:T(8,128)S(1)}, f32[32,256]{1,0:T(8,128)}, u32[]{:S(2)}) copy-start(f32[32,256]{1,0:T(8,128)} %bed_ref.1) | copy-start | bytes 98308
  4.2 0.8 %copy-start.4 = (f32[32,256]{1,0:T(8,128)S(1)}, f32[32,256]{1,0:T(8,128)}, u32[]{:S(2)}) copy-start(f32[32,256]{1,0:T(8,128)} %fdepth_ref.1) | copy-start | bytes 98308
  4.9 0.8 %copy-start.5 = (s32[32,256]{1,0:T(8,128)S(1)}, s32[32,256]{1,0:T(8,128)}, u32[]{:S(2)}) copy-start(s32[32,256]{1,0:T(8,128)} %wet_ref.1) | copy-start | bytes 98308
  5.7 0.8 %copy-start.6 = (s32[32,256]{1,0:T(8,128)S(1)}, s32[32,256]{1,0:T(8,128)}, u32[]{:S(2)}) copy-start(s32[32,256]{1,0:T(8,128)} %class_ref.1) | copy-start | bytes 98308
  6.4 0.7 %copy-start.7 = (s32[2048]{0:T(1024)S(1)}, s32[2048]{0:T(1024)}, u32[]{:S(2)}) copy-start(s32[2048]{0:T(1024)} %nest_ref.1) | copy-start | bytes 24580
  7.1 0.7 %copy-start.8 = (f32[11]{0:T(128)S(1)}, f32[11]{0:T(128)}, u32[]{:S(2)}) copy-start(f32[11]{0:T(128)} %manning_ref.1) | copy-start | bytes 136

commit v2 on v1

--- a/solution.py
+++ b/solution.py
@@ -82,16 +82,17 @@
 
 def kernel(
     nrow, ncol, nslots,
-    eta_ref, flux_ref, depth_ref, bed_ref, fdepth_ref, wet_ref, class_ref, manning_ref, nest_ref,
+    eta_ref, flux_ref, depth_ref, bed_ref, fdepth_ref, wet_ref, class_ref, manning_hbm, nest_hbm,
     out_eta, out_water, out_flux,
     ce, cs, pc, cl, cr, fe, pf, fl, fr, samp, sbuf, rbuf, acc,
-    send_sem, recv_sem, ssend_sem, srecv_sem,
+    fdepth, wet, kinds, manning, nest,
+    send_sem, recv_sem, ssend_sem, srecv_sem, load_sem,
 ):
     r = lax.axis_index("rows")
     c = lax.axis_index("cols")
     th, tw = eta_ref.shape
     fh = bed_ref.shape[0]
-    nb = nest_ref.shape[0]
+    nb = nest.shape[0]
     width = tw * ncol
     up, dn = r > 0, r < nrow - 1
     lf, rt = c > 0, c < ncol - 1
@@ -102,6 +103,14 @@
     ]
     arrives = [dn, up, rt, lf, dn & rt, dn & lf, up & rt, up & lf]
 
+    loads = [
+        (eta_ref, ce.at[0, PAD:PAD + th, 0:tw]),
+        (depth_ref, ce.at[1, PAD:PAD + th, 0:tw]),
+        (flux_ref, ce.at[2:4, PAD:PAD + th, 0:tw]),
+        (class_ref, kinds), (manning_hbm, manning), (wet_ref, wet), (fdepth_ref, fdepth),
+        (bed_ref, fe.at[1, PAD:PAD + fh, 0:tw]), (nest_hbm, nest),
+    ]
+    loads = [pltpu.make_async_copy(a, b, load_sem.at[i]) for i, (a, b) in enumerate(loads)]
     barrier = pltpu.get_barrier_semaphore()
     expected = jnp.int32(0)
     for there, rr, cc in around:
@@ -127,17 +136,22 @@
             sends = r > 0
         expected = expected + sends.astype(jnp.int32)
 
+    for load in loads:
+        load.start()
+
     def copies(ext, packed, left, right, high, base):
         a, b = PAD, PAD + high
+        n = packed.shape[0]
+        z = PAD + n
         whole = [
             (ext.at[:, a:a + PAD, 0:tw], ext.at[:, b:b + PAD, 0:tw]),
             (ext.at[:, b - PAD:b, 0:tw], ext.at[:, 0:a, 0:tw]),
-            (packed, right.at[a:b]),
-            (packed, left.at[a:b]),
-            (packed.at[0:PAD], right.at[b:b + PAD]),
-            (packed.at[0:PAD], left.at[b:b + PAD]),
-            (packed.at[high - PAD:high], right.at[0:PAD]),
-            (packed.at[high - PAD:high], left.at[0:PAD]),
+            (packed, right.at[PAD:z]),
+            (packed, left.at[PAD:z]),
+            (packed.at[0:PAD], right.at[z:z + PAD]),
+            (packed.at[0:PAD], left.at[z:z + PAD]),
+            (packed.at[n - PAD:n], right.at[0:PAD]),
+            (packed.at[n - PAD:n], left.at[0:PAD]),
         ]
         return [
             functools.partial(
@@ -151,8 +165,8 @@
     coarse_copies = copies(ce, pc, cl, cr, th, 0)
     fine_copies = copies(fe, pf, fl, fr, fh, 8)
 
-    def start(made):
-        for d in (2, 3, 0, 1, 4, 5, 6, 7):
+    def start(made, which):
+        for d in which:
             @pl.when(around[d][0])
             def _(d=d):
                 made[d]().start()
@@ -172,6 +186,7 @@
     def blank(ext, left, right, high):
         a, b = PAD, PAD + high
         fields = ext.shape[0]
+        z = left.shape[0] - PAD
 
         @pl.when(jnp.logical_not(up))
         def _():
@@ -182,8 +197,8 @@
         @pl.when(jnp.logical_not(dn))
         def _():
             ext[:, b:b + PAD, 0:tw] = jnp.zeros((fields, PAD, tw), jnp.float32)
-            left[b:b + PAD, :] = jnp.zeros((PAD, LANES), jnp.float32)
-            right[b:b + PAD, :] = jnp.zeros((PAD, LANES), jnp.float32)
+            left[z:z + PAD, :] = jnp.zeros((PAD, LANES), jnp.float32)
+            right[z:z + PAD, :] = jnp.zeros((PAD, LANES), jnp.float32)
 
         @pl.when(jnp.logical_not(lf))
         def _():
@@ -193,51 +208,71 @@
         def _():
             right[...] = jnp.zeros(right.shape, jnp.float32)
 
-    def pack(fields, reach):
+    def pack(fields, reach, fold):
         high = fields[0].shape[0]
-        lane = lax.broadcasted_iota(jnp.int32, (high, LANES), 1)
+        part = high // fold
+        step = 2 * reach * len(fields) if fold > 1 else 0
+        lane = lax.broadcasted_iota(jnp.int32, (part, LANES), 1)
         out = None
         for q, field in enumerate(fields):
-            edge = jnp.where(lane < LANES // 2, field[:, 0:LANES], field[:, tw - LANES:tw])
-            if q == 0:
-                out = edge
-            else:
-                lo = 2 * reach * q - reach
-                out = jnp.where((lane >= lo) & (lane < lo + 2 * reach), turn(edge, 2 * reach * q, 1), out)
+            edge = jnp.where(
+                lax.broadcasted_iota(jnp.int32, (high, LANES), 1) < LANES // 2,
+                field[:, 0:LANES], field[:, tw - LANES:tw],
+            )
+            for g in range(fold):
+                shift = g * step + 2 * reach * q
+                piece = edge[g * part:(g + 1) * part]
+                if shift == 0:
+                    out = piece
+                else:
+                    lo = shift - reach
+                    out = jnp.where((lane >= lo) & (lane < lo + 2 * reach), turn(piece, shift, 1), out)
         return out
 
-    def unpack(ext, left, right, reach):
+    def unpack(ext, left, right, reach, fold):
         lane = lax.broadcasted_iota(jnp.int32, left.shape, 1)
+        fields = ext.shape[0]
+        step = 2 * reach * fields if fold > 1 else 0
         of_right = lane < reach
-        for q in range(1, ext.shape[0]):
-            of_right = of_right | ((lane >= 2 * reach * q) & (lane < 2 * reach * q + reach))
+        for i in range(1, fields * fold):
+            of_right = of_right | ((lane >= 2 * reach * i) & (lane < 2 * reach * i + reach))
         merged = jnp.where(of_right, right[...], left[...])
-        for q in range(ext.shape[0]):
-            ext[q, :, tw:tw + LANES] = merged if q == 0 else turn(merged, -2 * reach * q, 1)
-
-    eta, depth = eta_ref[...], depth_ref[...]
-    f0, f1 = flux_ref[0], flux_ref[1]
-    for q, field in enumerate((eta, depth, f0, f1)):
-        ce[q, PAD:PAD + th, 0:tw] = field
-    pc[...] = pack((eta, depth, f0, f1), 2)
+        part = left.shape[0] - 2 * PAD
+        for q in range(fields):
+            pieces = [(0, PAD, fold - 1, 0), (PAD + part, part + 2 * PAD, 0, PAD + fold * part)]
+            pieces += [(PAD, PAD + part, g, PAD + g * part) for g in range(fold)]
+            for lo, hi, g, at in pieces:
+                shift = g * step + 2 * reach * q
+                piece = merged[lo:hi]
+                if shift:
+                    piece = turn(piece, -shift, 1)
+                ext[q, at:at + hi - lo, tw:tw + LANES] = piece
+
+    fold = th // 16
     blank(ce, cl, cr, th)
+    for load in loads[:3]:
+        load.wait()
     pl.semaphore_wait(barrier, expected)
-    start(coarse_copies)
-
-    kind = class_ref[...]
+    start(coarse_copies, (0, 1))
+    pc[...] = pack([ce[q, PAD:PAD + th, 0:tw] for q in range(4)], 2, fold)
+    start(coarse_copies, (2, 3, 4, 5, 6, 7))
+
+    for load in loads[3:]:
+        load.wait()
+    kind = kinds[...]
     rough = jnp.zeros(kind.shape, jnp.float32)
     for i in range(NCLASS):
-        rough = jnp.where(kind == i, manning_ref[i], rough)
-    water = wet_ref[...].astype(jnp.float32) * fdepth_ref[...]
-    bed = bed_ref[...]
-    for q, field in enumerate((water, bed, rough)):
-        fe[q, PAD:PAD + fh, 0:tw] = field
-    pf[...] = pack((water, bed, rough), FSTEPS)
+        rough = jnp.where(kind == i, manning[i], rough)
+    water = wet[...].astype(jnp.float32) * fdepth[...]
+    bed = fe[1, PAD:PAD + fh, 0:tw]
+    fe[0, PAD:PAD + fh, 0:tw] = water
+    fe[2, PAD:PAD + fh, 0:tw] = rough
+    pf[...] = pack((water, bed, rough), FSTEPS, 1)
     blank(fe, fl, fr, fh)
-    start(fine_copies)
+    start(fine_copies, (0, 1, 2, 3, 4, 5, 6, 7))
 
     wait_in(coarse_copies)
-    unpack(ce, cl, cr, 2)
+    unpack(ce, cl, cr, 2, fold)
     s, d, fa, fb = ce[0], ce[1], ce[2], ce[3]
     s, fa, fb = coarse_step(s, d, fa, fb)
     cs[0] = s[PAD:PAD + th, 0:tw]
@@ -253,7 +288,7 @@
     values = []
     for slot in range(nslots):
         seg = seg0 + slot * nrow
-        cell = nest_ref[jnp.minimum(seg * RATIO, nb - 1)]
+        cell = nest[jnp.minimum(seg * RATIO, nb - 1)]
         row = cell // width
         col = cell - row * width - c * tw
         row = row - r * th
@@ -282,12 +317,15 @@
             device_id=(0, c - k), device_id_type=MESH,
         )
 
+    def window_start(cc):
+        return jnp.maximum(cc * tw - FSTEPS, 0) // RATIO
+
+    lane_s = lax.broadcasted_iota(jnp.int32, (8, LANES), 1)
     for k in range(3):
-        at = place + (c - k) * tw
-        window = jnp.zeros((8, ext_w), jnp.float32)
+        at = lane_s + window_start(c - k)
+        window = jnp.zeros((8, LANES), jnp.float32)
         for slot in range(nslots):
-            begin = (seg0 + slot * nrow) * RATIO
-            window = jnp.where((at >= begin) & (at < begin + RATIO), values[slot], window)
+            window = jnp.where(at == seg0 + slot * nrow, values[slot], window)
         sbuf[k] = window
         sends = (r > 0) if k == 0 else (c - k >= 0)
 
@@ -296,7 +334,7 @@
             sample_copy(k).start()
 
     wait_in(fine_copies)
-    unpack(fe, fl, fr, FSTEPS)
+    unpack(fe, fl, fr, FSTEPS, 1)
 
     def keeps(high, first):
         row = lax.broadcasted_iota(jnp.int32, (high, ext_w), 0) + first
@@ -312,7 +350,7 @@
 
     @pl.when(r == 0)
     def _():
-        acc[...] = sbuf[0]
+        total = sbuf[0]
         for k in range(3):
             for rr in range(nrow):
                 if k == 0 and rr == 0:
@@ -326,7 +364,18 @@
                         send_sem=ssend_sem.at[k], recv_sem=srecv_sem.at[j],
                         device_id=(rr, c + k), device_id_type=MESH,
                     ).wait_recv()
-                    acc[...] += rbuf[j]
+        for k in range(3):
+            for rr in range(nrow):
+                if k == 0 and rr == 0:
+                    continue
+                total = total + jnp.where(c + k < ncol, rbuf[k * nrow + rr], 0.0)
+        first = window_start(c)
+        at = place + c * tw
+        spread = jnp.zeros((8, ext_w), jnp.float32)
+        for i in range((tw + 2 * FSTEPS) // RATIO + 2):
+            begin = (first + i) * RATIO
+            spread = jnp.where((at >= begin) & (at < begin + RATIO), total[:, i:i + 1], spread)
+        acc[...] = spread
         level_s = [acc[i:i + 1, :] for i in range(3)]
         still = acc[6:7, :]
         level_v = []
@@ -359,6 +408,17 @@
         @pl.when(sends)
         def _(k=k):
             sample_copy(k).wait_send()
+
+
+def deliver(a, b, c, to_a, to_b, to_c, sem):
+    moves = [
+        pltpu.make_async_copy(src, dst, sem.at[i])
+        for i, (src, dst) in enumerate(((a, to_a), (b, to_b), (c, to_c)))
+    ]
+    for move in moves:
+        move.start()
+    for move in moves:
+        move.wait()
 
 
 def per_device(nrow, ncol, *args):
@@ -371,40 +431,54 @@
     span = max((tw + REACH) // RATIO + 1, segments - last_low)
     nslots = -(-span // nrow)
     vmem = pl.BlockSpec(memory_space=pltpu.VMEM)
-    smem = pl.BlockSpec(memory_space=pltpu.SMEM)
+    hbm = pl.BlockSpec(memory_space=pltpu.HBM)
     f32 = jnp.float32
-    return pl.pallas_call(
+    shapes = (
+        jax.ShapeDtypeStruct((th, tw), f32),
+        jax.ShapeDtypeStruct((fh, tw), f32),
+        jax.ShapeDtypeStruct((2, fh, tw), f32),
+    )
+    outs = pl.pallas_call(
         functools.partial(kernel, nrow, ncol, nslots),
-        out_shape=(
-            jax.ShapeDtypeStruct((th, tw), f32),
-            jax.ShapeDtypeStruct((fh, tw), f32),
-            jax.ShapeDtypeStruct((2, fh, tw), f32),
-        ),
-        in_specs=[vmem] * 7 + [smem] * 2,
+        out_shape=shapes,
+        in_specs=[hbm] * 9,
         out_specs=(vmem, vmem, vmem),
         scratch_shapes=[
             pltpu.VMEM((4, th + 2 * PAD, ext_w), f32),
             pltpu.VMEM((4, th, tw), f32),
-            pltpu.VMEM((th, LANES), f32),
-            pltpu.VMEM((th + 2 * PAD, LANES), f32),
-            pltpu.VMEM((th + 2 * PAD, LANES), f32),
+            pltpu.VMEM((16, LANES), f32),
+            pltpu.VMEM((16 + 2 * PAD, LANES), f32),
+            pltpu.VMEM((16 + 2 * PAD, LANES), f32),
             pltpu.VMEM((3, fh + 2 * PAD, ext_w), f32),
             pltpu.VMEM((fh, LANES), f32),
             pltpu.VMEM((fh + 2 * PAD, LANES), f32),
             pltpu.VMEM((fh + 2 * PAD, LANES), f32),
             pltpu.VMEM((nslots * 8, tw), f32),
-            pltpu.VMEM((3, 8, ext_w), f32),
-            pltpu.VMEM((3 * nrow, 8, ext_w), f32),
+            pltpu.VMEM((3, 8, LANES), f32),
+            pltpu.VMEM((3 * nrow, 8, LANES), f32),
             pltpu.VMEM((8, ext_w), f32),
+            pltpu.VMEM((fh, tw), f32),
+            pltpu.VMEM((fh, tw), jnp.int32),
+            pltpu.VMEM((fh, tw), jnp.int32),
+            pltpu.SMEM(manning.shape, f32),
+            pltpu.SMEM(nest_map.shape, jnp.int32),
             pltpu.SemaphoreType.DMA((16,)),
             pltpu.SemaphoreType.DMA((16,)),
             pltpu.SemaphoreType.DMA((3,)),
             pltpu.SemaphoreType.DMA((3 * nrow,)),
+            pltpu.SemaphoreType.DMA((9,)),
         ],
         compiler_params=pltpu.CompilerParams(
-            collective_id=0, has_side_effects=True, vmem_limit_bytes=32 * 1024 * 1024
+            collective_id=0, has_side_effects=True, vmem_limit_bytes=60 * 1024 * 1024
         ),
     )(*args)
+    return pl.pallas_call(
+        deliver,
+        out_shape=shapes,
+        in_specs=[hbm] * 3,
+        out_specs=(hbm, hbm, hbm),
+        scratch_shapes=[pltpu.SemaphoreType.DMA((3,))],
+    )(*outs)
 
 
 def solution(mesh):

time: 25.9 us -> 24.4 us (0.942); the launches traced: 25.4 us -> 24.3 us
  local copies, waits for them, and re-layouts: 9.03 us -> 0 us
  Pallas kernels: 15.7 us -> 23.6 us
    unnamed x21 -> x0, local copies, waits for them, and re-layouts: 9.03 us -> none
    pallas_call x1 -> x2, Pallas kernels: 15.7 us -> 23.6 us  [the longest x1 15.5 us: per_device(): pl.pallas_call(functools.partial(kernel, nrow, ncol, nslots), out_shape=s...]
where the time goes in v2:
time: 24.4 us; the launch traced here: 24.3 us
  Pallas kernels  23.6 us (97%)
  between operations  0.64 us (3%)
    pallas_call x1, Pallas kernels, per_device(): pl.pallas_call(functools.partial(kernel, nrow, ncol, nslots), out_shape=s...  15.5 us
    pallas_call x1, Pallas kernels, per_device(): pl.pallas_call(deliver, out_shape=shapes, in_specs=[hbm] * 3, out_specs=(...  8.08 us

profile of v2, /device:TPU:0, one launch (start us, length us, event | category | flops | bytes accessed | tf_op | source)
XLA Modules:
  0.0 24.3 jit_solution(10295864661915258038)
XLA Ops:
  0.6 15.5 %shard_map.112 = (f32[128,256]{1,0:T(8,128)}, f32[32,256]{1,0:T(8,128)}, f32[2,32,256]{2,1,0:T(8,128)}) custom-call(f32[128,256]{1,0:T(8,128)} %eta_ref.1, f32[2,128,256]{2,1,0:T(8,128)} %flux_ref.1, f32[128,256]{1,0:T(8,128)} %depth_ref.1, f32[32,256]{1,0:T(8,128)} %bed_ref.1, f32[32,256]{1,0:T(8,128)} %fdepth_ref.1, s32[32,256]{1,0:T(8,128)} %wet_ref.1, ...), custom_call_target="tpu_custom_call" | custom-call | tf_op jit(solution)/shard_map/pallas_call | solution.py:441
  16.2 8.1 %shard_map.113 = (f32[128,256]{1,0:T(8,128)}, f32[32,256]{1,0:T(8,128)}, f32[2,32,256]{2,1,0:T(8,128)}) custom-call(f32[128,256]{1,0:T(8,128)} %get-tuple-element.6.a, f32[32,256]{1,0:T(8,128)} %get-tuple-element.7.b, f32[2,32,256]{2,1,0:T(8,128)} %get-tuple-element.8.c), custom_call_target="tpu_custom_call" | custom-call | tf_op jit(solution)/shard_map/pallas_call | solution.py:475

commit v3 on v2

--- a/solution.py
+++ b/solution.py
@@ -46,7 +46,7 @@
     return surf, new_rows, new_cols
 
 
-def fine_run(water, bed, rough, row_keep, col_keep, top):
+def fine_run(water, bed, rough, row_keep, col_keep, top, steps=FSTEPS):
     bed_faces = [jnp.maximum(bed, turn(bed, -1, axis)) for axis in (0, 1)]
     drag = []
     for axis in (0, 1):
@@ -55,7 +55,7 @@
     keep = (row_keep, col_keep)
     flux = [None, None]
     first_row = lax.broadcasted_iota(jnp.int32, water.shape, 0) == 0
-    for step in range(FSTEPS):
+    for step in range(steps):
         surf = bed + water
         new = []
         for axis in (0, 1):
@@ -440,7 +440,7 @@
     )
     outs = pl.pallas_call(
         functools.partial(kernel, nrow, ncol, nslots),
-        out_shape=shapes,
+        out_shape=tuple(pltpu.VMEM(x.shape, f32) for x in shapes),
         in_specs=[hbm] * 9,
         out_specs=(vmem, vmem, vmem),
         scratch_shapes=[
@@ -472,10 +472,11 @@
             collective_id=0, has_side_effects=True, vmem_limit_bytes=60 * 1024 * 1024
         ),
     )(*args)
+    outs = [pltpu.with_memory_space_constraint(x, pltpu.VMEM) for x in outs]
     return pl.pallas_call(
         deliver,
         out_shape=shapes,
-        in_specs=[hbm] * 3,
+        in_specs=[vmem] * 3,
         out_specs=(hbm, hbm, hbm),
         scratch_shapes=[pltpu.SemaphoreType.DMA((3,))],
     )(*outs)

time: 24.4 us -> 16.4 us (0.67)
  Pallas kernels: 23.6 us -> 15.6 us
    pallas_call x2, Pallas kernels: 23.6 us -> 15.6 us  [the longest x1 14.8 us: per_device(): pl.pallas_call(functools.partial(kernel, nrow, ncol, nslots), out_shape=t...]
where the time goes in v3:
time: 16.4 us; the launch traced here: 16.2 us
  Pallas kernels  15.6 us (95%)
  between operations  0.64 us (4%)
    pallas_call x1, Pallas kernels, per_device(): pl.pallas_call(functools.partial(kernel, nrow, ncol, nslots), out_shape=t...  14.8 us
    pallas_call x1, Pallas kernels, per_device(): pl.pallas_call(deliver, out_shape=shapes, in_specs=[vmem] * 3, out_specs=...  0.71 us

profile of v3, /device:TPU:0, one launch (start us, length us, event | category | flops | bytes accessed | tf_op | source)
XLA Modules:
  0.0 16.2 jit_solution(8747920070980978518)
XLA Ops:
  0.6 14.8 %shard_map.112 = (f32[128,256]{1,0:T(8,128)S(1)}, f32[32,256]{1,0:T(8,128)S(1)}, f32[2,32,256]{2,1,0:T(8,128)S(1)}) custom-call(f32[128,256]{1,0:T(8,128)} %eta_ref.1, f32[2,128,256]{2,1,0:T(8,128)} %flux_ref.1, f32[128,256]{1,0:T(8,128)} %depth_ref.1, f32[32,256]{1,0:T(8,128)} %bed_ref.1, f32[32,256]{1,0:T(8,128)} %fdepth_ref.1, s32[32,256]{1,0:T(8,128)} %wet_ref.1, ...), custom_call_target="tpu_custom_call" | custom-call | tf_op jit(solution)/shard_map/pallas_call | solution.py:441
  15.5 0.7 %shard_map.113 = (f32[128,256]{1,0:T(8,128)}, f32[32,256]{1,0:T(8,128)}, f32[2,32,256]{2,1,0:T(8,128)}) custom-call(f32[128,256]{1,0:T(8,128)S(1)} %get-tuple-element.6.a, f32[32,256]{1,0:T(8,128)S(1)} %get-tuple-element.7.b, f32[2,32,256]{2,1,0:T(8,128)S(1)} %get-tuple-element.8.c), custom_call_target="tpu_custom_call" | custom-call | tf_op jit(solution)/shard_map/pallas_call | solution.py:476
